TPU v7x, 32 devices: a whole 2x2x4 slice. The times are simulated.
32 devices in a mesh: grp: 2 (over y), neur: 16 (over z, x, core).
Axes of the slice: x: 2, y: 2, z: 4, core: 2. Of those that a mesh axis runs over, the one named last changes fastest.
Arguments:
- activations: bfloat16 [48, 3584], P('grp', 'neur'), parts along dimension 0, may hold values from -6 to 6
- residual: bfloat16 [48, 8192], P('grp'), parts along dimension 0, may hold values from -6 to 6
- down_weight: bfloat16 [3584, 8192], P('neur'), may hold values from -0.09375 to 0.09375
- norm_gain: bfloat16 [8192], replicated, may hold values from 0.5 to 1.5
- lens_weight: bfloat16 [1024, 8192], P('neur')
- targets: int32 [48], P('grp'), parts along dimension 0, may hold values from 0 to 1023
Outputs:
- attribution: float32 [48, 3584], P('grp', 'neur'), parts along dimension 0
- target_logprob: float32 [48, 20], P('grp'), parts along dimension 0
There are 2 independent parts, one for each index of `grp`. A program takes and returns all parts, laid end to end along the dimension named above; an argument that names none is the same for every part. Nothing has to cross between parts.
All inputs are finite; a program needn't handle non-finite values.
Results may differ from a plain program's by a relative error of at most 0.007.
Values may be sent and summed in bfloat16 or wider, within the bound.
A program may use at most 64 MiB of HBM per device.

v0:
```python
import jax
import jax.numpy as jnp
from jax import lax
from jax.sharding import PartitionSpec as P

STEPS = 20


EPS = 1e-05


def local(activations, residual, down_weight, norm_gain, lens_weight, targets):
    prompt_rows, model_width = residual.shape
    vocab_rows = lens_weight.shape[0]
    stream_base = residual.astype(jnp.float32)
    gain_vector = norm_gain.astype(jnp.float32)
    column_piece = lax.psum_scatter(
        lax.dot_general(
            down_weight, activations, (((0,), (1,)), ((), ())), preferred_element_type=jnp.float32
        ),
        "neur",
        scatter_dimension=0,
        tiled=True,
    )
    update = lax.all_gather(column_piece, "neur", axis=0, tiled=True).T
    alphas = (jnp.arange(STEPS, dtype=jnp.float32) + 1.0) / STEPS

    def forward(alpha_block):
        stream = stream_base[None] + alpha_block[:, None, None] * update[None]
        root_mean = jnp.sqrt(jnp.mean(stream * stream, axis=2) + EPS)
        normed = (gain_vector * stream / root_mean[..., None]).astype(jnp.bfloat16)
        logits = jnp.einsum("kpd,vd->kpv", normed, lens_weight, preferred_element_type=jnp.float32)
        return (logits, root_mean)

    logits, root_mean = lax.map(forward, alphas.reshape(STEPS // 4, 4))
    logits = logits.reshape(STEPS, prompt_rows, vocab_rows)
    root_mean = root_mean.reshape(STEPS, prompt_rows)
    vocab_start = lax.axis_index("neur") * vocab_rows
    onehot = (
        jnp.arange(vocab_rows, dtype=jnp.int32)[None, :] + vocab_start == targets[:, None]
    ).astype(jnp.float32)
    local_peak = jnp.max(logits, axis=2)
    target_hit = jnp.sum(logits * onehot[None], axis=2)
    row_peak = lax.pmax(local_peak, "neur")
    exp_total, chosen = lax.psum(
        (jnp.sum(jnp.exp(logits - row_peak[..., None]), axis=2), target_hit), "neur"
    )
    logprob = chosen - row_peak - jnp.log(exp_total)
    residue = onehot[None] - jnp.exp(logits - row_peak[..., None]) / exp_total[..., None]
    local_curv = jnp.sum(residue * logits, axis=2)
    coefficient = jnp.sum(residue / root_mean[..., None], axis=0).astype(jnp.bfloat16)
    back, curvature = lax.psum(
        (jnp.dot(coefficient, lens_weight, preferred_element_type=jnp.float32), local_curv), "neur"
    )
    weight = curvature / (model_width * root_mean * root_mean)
    first_sum = jnp.sum(weight, axis=0)
    second = jnp.sum(weight * alphas[:, None], axis=0)
    grad_sum = (
        gain_vector * back - first_sum[:, None] * stream_base - second[:, None] * update
    ).astype(jnp.bfloat16)
    projected = lax.dot_general(
        grad_sum, down_weight, (((1,), (1,)), ((), ())), preferred_element_type=jnp.float32
    )
    attribution = 16.0 / STEPS * activations.astype(jnp.float32) * projected
    return (attribution, logprob.T)


def solution(mesh):
    placed = (P("grp", "neur"), P("grp", None), P("neur", None), P(), P("neur", None), P("grp"))
    return jax.shard_map(
        local,
        mesh=mesh,
        in_specs=placed,
        out_specs=(P("grp", "neur"), P("grp", None)),
        check_vma=False,
    )
```

profile of v0, /device:TPU:1, one launch (start us, length us, event | category | flops | bytes accessed | tf_op | source)
XLA Modules:
  0.0 317.1 jit_solution(7429235019826947538)
XLA Ops:
  7.2 0.0 reduce-scatter.2.cloned.1.call-start
  7.3 3.6 %fusion.15 = f32[8192,24]{0,1:T(8,128)} fusion(bf16[224,8192]{1,0:T(8,128)(2,1)} %param.10, bf16[24,224]{1,0:T(8,128)(2,1)} %param.8), kind=kOutput, calls=%fused_computation.35 | convolution fusion | flops 88080384 | bytes 4467200 | tf_op jit(solution)/shard_map/dot_general | solution.py:18
  10.9 0.0 reduce-scatter.2.cloned.1.call-update
  10.9 0.0 all-reduce.3.cloned.1.call-start
  11.0 0.1 convert_element_type.28
  11.1 0.1 compare_convert_fusion
  11.2 57.2 %reduce-scatter.2.cloned.1.call-done = f32[512,24]{0,1:T(8,128)} async-done(((f32[8192,24]{0,1:T(8,128)}), f32[512,24]{0,1:T(8,128)}) %reduce-scatter.2.cloned.1.call-update) | async-done | bytes 49168 | tf_op jit(solution)/shard_map/reduce_scatter | solution.py:17
  68.4 24.2 %all_gather.3 = f32[8192,24]{0,1:T(8,128)S(1)} all-gather(f32[512,24]{0,1:T(8,128)} %reduce-scatter.2.cloned.1.call-done), channel_id=1, replica_groups=mesh['grp'=2,'neur'=16] {'neur'}, dimensions={0}, use_global_device_ids=true | all-gather | bytes 835584 | tf_op jit(solution)/shard_map/all_gather | solution.py:25
  92.6 8.0 %while.12 = (s32[]{:T(128)}, f32[5,4,24,64]{3,2,1,0:T(8,128)S(1)}, f32[5,4,24]{2,1,0:T(4,128)S(1)}, f32[8192]{0:T(1024)S(1)}, f32[24,8192]{1,0:T(8,128)S(1)}, /*...) while((s32[]{:T(128)}, f32[5,4,24,64]{3,2,1,0:T(8,128)S(1)}, ...), condition=%wide.region_3.4_spmd, body=%wide.region_1.3_spmd.sunk | while | flops 107741472 | bytes 4284193 | solution.py:35
  92.6 0.6 multiply_reduce_fusion.5
  93.2 0.9 fusion.27
  94.2 0.6 multiply_reduce_fusion.5
  94.8 0.9 fusion.27
  95.8 0.6 multiply_reduce_fusion.5
  96.4 0.9 fusion.27
  97.4 0.6 multiply_reduce_fusion.5
  98.0 0.9 fusion.27
  99.0 0.6 multiply_reduce_fusion.5
  99.7 0.9 fusion.27
  100.6 0.0 copy-start.2
  100.6 0.1 reduce_max.11
  100.8 53.0 %pmax.7 = f32[20,24]{1,0:T(8,128)S(1)} all-reduce(f32[20,24]{1,0:T(8,128)S(1)} %reduce_max.12), channel_id=1, replica_groups=mesh['grp'=2,'neur'=16] {'neur'}, use_global_device_ids=true, to_apply=%region_5.6 | all-reduce | flops 480 | bytes 3840 | tf_op jit(solution)/shard_map/pmax | solution.py:44
  153.7 0.3 fusion.8
  154.0 57.6 %psum.28 = f32[20,24]{1,0:T(8,128)S(1)} all-reduce(f32[20,24]{1,0:T(8,128)S(1)} %reduce_sum.70), channel_id=1, replica_groups=mesh['grp'=2,'neur'=16] {'neur'}, use_global_device_ids=true, to_apply=%region_7.8 | all-reduce | flops 480 | bytes 3840 | tf_op jit(solution)/shard_map/psum | solution.py:45
  211.7 0.5 multiply_reduce_fusion.2
  212.1 1.2 fusion.16
  213.3 0.0 all-reduce.3.cloned.1.call-update
  213.4 57.9 %all-reduce = (f32[20,24]{1,0:T(8,128)S(1)}, f32[20,24]{1,0:T(8,128)S(1)}) all-reduce(f32[20,24]{1,0:T(8,128)S(1)} %reduce_sum.73, f32[20,24]{1,0:T(8,128)S(1)} %reduce_sum.77), channel_id=1, replica_groups=mesh['grp'=2,'neur'=16] {'neur'}, use_global_device_ids=true, to_apply=%region_11.12 | all-reduce | flops 960 | bytes 7680 | tf_op jit(solution)/shard_map/psum | solution.py:52
  271.3 0.1 fusion.14
  271.4 0.7 copy.10
  272.0 34.3 %all-reduce.3.cloned.1.call-done = f32[24,8192]{1,0:T(8,128)} async-done(((f32[24,8192]{1,0:T(8,128)}), f32[24,8192]{1,0:T(8,128)}) %all-reduce.3.cloned.1.call-update) | async-done | bytes 786448 | tf_op jit(solution)/shard_map/psum | solution.py:52
  306.3 4.0 %convolution_multiply_fusion = f32[24,224]{1,0:T(8,128)} fusion(bf16[224,8192]{1,0:T(8,128)(2,1)} %param.10, f32[24,8192]{1,0:T(8,128)} %all-reduce.3.cloned.1.call-done, f32[24]{0:T(128)S(1)} %get-tuple-element.53, f32[24]{0:T(128)S(1)} %get-tuple-element.52, f32[8192]{0:T(1024)S(1)} %get-tuple-element.158, bf16[24,8192]{1,0:T(8,128)(2,1)S(1)} %copy-done, ...), kind=kOutput, calls=%fused_computation.11 | convolution fusion | flops 89472768 | bytes 5701312 | tf_op jit(solution)/shard_map/dot_general | solution.py:61
  (37 shorter events, 0.3 us)
Async XLA Ops:
  7.2 3.8 %copy-start.3 = (bf16[8192]{0:T(1024)(128)(2,1)S(1)}, bf16[8192]{0:T(1024)(128)(2,1)}, u32[]{:S(2)}) copy-start(bf16[8192]{0:T(1024)(128)(2,1)} %param.11) | copy-start | bytes 49156
  7.2 3.8 %copy-start = (bf16[24,8192]{1,0:T(8,128)(2,1)S(1)}, bf16[24,8192]{1,0:T(8,128)(2,1)}, u32[]{:S(2)}) copy-start(bf16[24,8192]{1,0:T(8,128)(2,1)} %param.9) | copy-start | bytes 1179652
  7.2 3.9 %copy-start.4 = (s32[24]{0:T(128)S(1)}, s32[24]{0:T(128)}, u32[]{:S(2)}) copy-start(s32[24]{0:T(128)} %param.13) | copy-start | bytes 292
  7.2 85.4 %copy-start.1 = (bf16[64,8192]{1,0:T(8,128)(2,1)S(1)}, bf16[64,8192]{1,0:T(8,128)(2,1)}, u32[]{:S(2)}) copy-start(bf16[64,8192]{1,0:T(8,128)(2,1)} %param.12) | copy-start | bytes 3145732
  7.2 61.1 %reduce-scatter.2.cloned.1.call-start = ((), (), s32[]{:S(2)}) async-start(), calls=%async_computation.1 | async-start | bytes 835584 | tf_op jit(solution)/shard_map/reduce_scatter | solution.py:17
  10.9 295.4 %all-reduce.3.cloned.1.call-start = ((), (), s32[]{:S(2)}) async-start(), calls=%async_computation.2 | async-start | bytes 1572864 | tf_op jit(solution)/shard_map/psum | solution.py:52
  100.6 205.7 %copy-start.2 = (bf16[24,224]{1,0:T(8,128)(2,1)S(1)}, bf16[24,224]{1,0:T(8,128)(2,1)}, u32[]{:S(2)}) copy-start(bf16[24,224]{1,0:T(8,128)(2,1)} %param.8) | copy-start | bytes 32260
Sparse Core Ops, SparseCore 0:
  11.6 56.7 reduce-scatter.1
  213.4 92.8 all-reduce.2
where the time goes:
time: 319 us; the launch traced here: 317 us
  blocking collectives  193 us (61%)
  waiting for transfers between devices  91.5 us (29%)
  between operations  14.2 us (4%)
  matrix products  13.3 us (4%)
  other arithmetic  4.44 us (1%)
    psum x1, blocking collectives, local(): lax.psum((jnp.dot(coefficient, lens_weight, preferred_element_type=jnp.fl...  57.9 us
    psum x1, blocking collectives, local(): lax.psum((jnp.sum(jnp.exp(logits - row_peak[..., None]), axis=2), target_...  57.6 us
    reduce_scatter x1, waiting for transfers between devices, local(): lax.psum_scatter(lax.dot_general(down_weight, activations, (((0,), (1,)),...  57.2 us
    pmax x1, blocking collectives, local(): row_peak = lax.pmax(local_peak, 'neur')  53 us
    psum x1, waiting for transfers between devices, local(): lax.psum((jnp.dot(coefficient, lens_weight, preferred_element_type=jnp.fl...  34.3 us
    all_gather x1, blocking collectives, local(): update = lax.all_gather(column_piece, 'neur', axis=0, tiled=True).T  24.2 us
  transfers between devices with their start and end apart: 2, of which 2 were waited for; matrix products, arithmetic and copies ran while one was open for 0% of the time, Pallas kernels for 0%

commit v1 on v0

v1 whole, which is shorter than its diff:
```python
import functools

import jax
import jax.numpy as jnp
from jax import lax
from jax.experimental import pallas as pl
from jax.experimental.pallas import tpu as pltpu
from jax.sharding import PartitionSpec as P

MESH = pl.DeviceIdType.MESH
STEPS = 20
EPS = 1e-05
F32, BF16 = jnp.float32, jnp.bfloat16
LANES, GROUP = 128, 32


def nt(x, y):
    return lax.dot_general(x, y, (((1,), (1,)), ((), ())), preferred_element_type=F32)


def loop(count, body):
    if count <= 8:
        for index in range(count):
            body(index)
    else:
        pl.loop(0, count)(body)


def pack(x):
    rows, cols = x.shape
    if cols % 256 == 0:
        return jnp.concatenate([x[:, : cols // 2], x[:, cols // 2 :]], axis=0).astype(BF16)
    return jnp.concatenate([x, jnp.zeros((-rows % 16, cols), F32)], axis=0).astype(BF16)


def unpack(y, rows):
    y = y.astype(F32)
    if y.shape[0] == 2 * rows:
        return jnp.concatenate([y[:rows], y[rows:]], axis=1)
    return y[:rows]


def kernel(n, p, q, act, res, gain, tgt, down_hbm, lens_hbm, attr, logp,
           down, lens, acc, acc2, s1, r1, s2, r2, s3, r3, ug, gg, st, ebuf, mats,
           load_sem, rs_send, rs_recv, ag_send, ag_recv):
    m = p * q
    rows, width = res.shape
    vocab = lens.shape[0]
    blk = width // n
    grp, me = lax.axis_index("grp"), lax.axis_index("neur")
    core = lax.rem(me, 2)
    qi = lax.rem(me // 2, q)
    pi = me // (2 * q)
    other = 1 - core
    mine = core * m + qi * p + pi

    loads = []
    for slot, half in enumerate((other, core)):
        cols = pl.ds(pl.multiple_of(half * (width // 2), width // 2), width // 2)
        loads.append(pltpu.make_async_copy(down_hbm.at[:, cols], down.at[:, cols], load_sem.at[slot]))
    loads.append(pltpu.make_async_copy(lens_hbm, lens, load_sem.at[2]))
    for load in loads:
        load.start()

    def dev(p_at, q_at, c_at):
        return (grp, (p_at * q + q_at) * 2 + c_at)

    core_peer = dev(pi, qi, other)
    q_at = [lax.rem(qi + o, q) for o in range(1, q)]
    p_at = [lax.rem(pi + o, p) for o in range(1, p)]
    q_peers = [dev(pi, at, core) for at in q_at]
    p_peers = [dev(at, qi, core) for at in p_at]
    barrier = pltpu.get_barrier_semaphore()
    peers = [core_peer] + q_peers + p_peers
    for peer in peers:
        pl.semaphore_signal(barrier, inc=1, device_id=peer, device_id_type=MESH)
    pl.semaphore_wait(barrier, len(peers))

    sent = []

    def send(src, dst, send_sem, recv_sem, peer):
        copy = pltpu.make_async_remote_copy(
            src_ref=src, dst_ref=dst, send_sem=send_sem, recv_sem=recv_sem,
            device_id=peer, device_id_type=MESH)
        copy.start()
        sent.append(copy)
        return copy

    def cols_of(b):
        return pl.ds(pl.multiple_of(b * blk, blk), blk)

    def reduce_scatter(rd, part, before, between, filler):
        ss, rs = rs_send.at[rd], rs_recv.at[rd]

        def away(j):
            s1[rd, j] = pack(part(other * m + j))

        before()
        loop(m, away)
        first = send(s1.at[rd], r1.at[rd], ss.at[0], rs.at[0], core_peer)
        between()

        def keep(j):
            acc[j] = part(core * m + j)

        loop(m, keep)
        filler()
        first.wait_recv()

        def halved(j):
            return acc[j] + unpack(r1[rd, j], rows)

        copies = []
        for o, (at, peer) in enumerate(zip(q_at, q_peers)):
            for i in range(p):
                s2[rd, o, i] = pack(halved(at * p + i))
            copies.append(send(s2.at[rd, o], r2.at[rd, o], ss.at[1 + o], rs.at[1 + o], peer))
        for i in range(p):
            acc2[i] = halved(qi * p + i)
        for copy in copies:
            copy.wait_recv()

        def quartered(i):
            total = acc2[i]
            for o in range(q - 1):
                total = total + unpack(r2[rd, o, i], rows)
            return total

        copies = []
        for o, (at, peer) in enumerate(zip(p_at, p_peers)):
            s3[rd, o] = pack(quartered(at))
            copies.append(send(s3.at[rd, o], r3.at[rd, o], ss.at[q + o], rs.at[q + o], peer))
        total = quartered(pi)
        for copy in copies:
            copy.wait_recv()
        for o in range(p - 1):
            total = total + unpack(r3[rd, o], rows)
        return total

    def all_gather(rd, buf):
        ss, rs = ag_send.at[rd], ag_recv.at[rd]
        copies = [send(buf.at[mine], buf.at[mine], ss.at[o], rs.at[o], peer)
                  for o, peer in enumerate(p_peers)]
        for copy in copies:
            copy.wait_recv()
        part = buf.at[pl.ds(core * m + qi * p, p)]
        copies = [send(part, part, ss.at[p - 1 + o], rs.at[p - 1 + o], peer)
                  for o, peer in enumerate(q_peers)]
        for copy in copies:
            copy.wait_recv()
        part = buf.at[pl.ds(core * m, m)]
        send(part, part, ss.at[p + q - 2], rs.at[p + q - 2], core_peer).wait_recv()

    def split(x):
        high = x.astype(BF16).astype(F32)
        return jnp.concatenate([high, x - high], axis=0).astype(BF16)

    activations = act[...]

    def update_part(b):
        return jnp.dot(activations, down[:, cols_of(b)], preferred_element_type=F32)

    def lane_sum(x):
        total = x[:, :LANES]
        for at in range(LANES, x.shape[1], LANES):
            total = total + x[:, at : at + LANES]
        return total

    mats[...] = jnp.zeros_like(mats)
    acc_a, acc_b = mats.at[0], mats.at[1]
    sq_rr, sq_ru, sq_uu = (mats.at[2 + i, pl.ds(0, rows)] for i in range(3))

    def residual_terms():
        loads[2].wait()

        def body(b):
            base = res[:, cols_of(b)].astype(F32)
            sq_rr[...] += lane_sum(base * base)
            acc_a[:, :vocab] += nt(split(gain[:, cols_of(b)] * base), lens[:, cols_of(b)])

        loop(n, body)

    with jax.named_scope("update_sum"):
        update = reduce_scatter(0, update_part, loads[0].wait, loads[1].wait, residual_terms)
    ug[mine] = pack(update)
    with jax.named_scope("update_gather"):
        all_gather(0, ug)

    def update_terms(b):
        base = res[:, cols_of(b)].astype(F32)
        up = unpack(ug[b], rows)
        sq_ru[...] += lane_sum(base * up)
        sq_uu[...] += lane_sum(up * up)
        acc_b[:, :vocab] += nt(split(gain[:, cols_of(b)] * up), lens[:, cols_of(b)])

    loop(n, update_terms)

    with jax.named_scope("softmax_parts"):
        a_log = acc_a[:rows, :vocab] + acc_a[rows:, :vocab]
        b_log = acc_b[:rows, :vocab] + acc_b[rows:, :vocab]
        rr = jnp.sum(sq_rr[...], axis=1, keepdims=True) * (1.0 / width)
        ru = jnp.sum(sq_ru[...], axis=1, keepdims=True) * (2.0 / width)
        uu = jnp.sum(sq_uu[...], axis=1, keepdims=True) * (1.0 / width)
        lane = lax.broadcasted_iota(jnp.int32, (rows, LANES), 1)
        alphas = (lane + 1).astype(F32) / STEPS
        live = lane < STEPS
        inv_root = 1.0 / jnp.sqrt(rr + alphas * ru + alphas * alphas * uu + EPS)
        inv_root = jnp.where(live, inv_root, 0.0)
        hit = lax.broadcasted_iota(jnp.int32, (rows, vocab), 1) + me * vocab == tgt[...]
        a_hit = jnp.sum(jnp.where(hit, a_log, 0.0), axis=1, keepdims=True)
        b_hit = jnp.sum(jnp.where(hit, b_log, 0.0), axis=1, keepdims=True)
        chosen = (a_hit + alphas * b_hit) * inv_root
        peaks = jnp.zeros((rows, LANES), F32)
        packed = pltpu.roll(chosen, 3 * GROUP, 1)
        for k in range(STEPS):
            logits = (a_log + ((k + 1) / STEPS) * b_log) * inv_root[:, k : k + 1]
            peak = jnp.max(logits, axis=1, keepdims=True)
            grown = jnp.exp(logits - peak)
            ebuf[k] = grown
            peaks = jnp.where(lane == k, peak, peaks)
            packed = jnp.where(lane == GROUP + k, jnp.sum(grown, axis=1, keepdims=True), packed)
            packed = jnp.where(lane == 2 * GROUP + k, jnp.sum(grown * logits, axis=1, keepdims=True), packed)
        st[mine] = jnp.where(lane < GROUP, peaks, packed)
    with jax.named_scope("softmax_gather"):
        all_gather(1, st)

    with jax.named_scope("softmax_whole"):
        top = st[0]
        for b in range(1, n):
            top = jnp.maximum(top, st[b])
        total = jnp.zeros((rows, LANES), F32)
        moment = jnp.zeros((rows, LANES), F32)
        plain = jnp.zeros((rows, LANES), F32)
        for b in range(n):
            x = st[b]
            factor = jnp.exp(x - top)
            total += factor * pltpu.roll(x, 3 * GROUP, 1)
            moment += factor * pltpu.roll(x, 2 * GROUP, 1)
            plain += x
        total = jnp.where(live, total, 1.0)
        chosen = pltpu.roll(plain, GROUP, 1)
        logp[...] = (chosen - top - jnp.log(total))[:, :STEPS]
        weight = (chosen - moment / total) * inv_root * inv_root * (1.0 / width)
        weight = jnp.where(live, weight, 0.0)
        first_sum = jnp.sum(weight, axis=1, keepdims=True)
        second_sum = jnp.sum(weight * alphas, axis=1, keepdims=True)
        scale = jnp.where(live, jnp.exp(peaks - top), 0.0) / total * inv_root
        coefficient = jnp.where(hit, jnp.sum(inv_root, axis=1, keepdims=True), 0.0)
        for k in range(STEPS):
            coefficient = coefficient - ebuf[k] * scale[:, k : k + 1]
        coefficient = coefficient.astype(BF16)

    def back_part(b):
        return jnp.dot(coefficient, lens[:, cols_of(b)], preferred_element_type=F32)

    def nothing():
        return None

    with jax.named_scope("back_sum"):
        back = reduce_scatter(1, back_part, nothing, nothing, nothing)
    own = cols_of(mine)
    gg[mine] = pack(gain[:, own] * back - first_sum * res[:, own].astype(F32) - second_sum * update)
    with jax.named_scope("gradient_gather"):
        all_gather(2, gg)

    with jax.named_scope("projection"):
        folds = gg.shape[1] // rows
        step = gg.shape[2]
        neurons = down.shape[0]
        proj = jnp.zeros((rows, neurons), F32)
        for b in range(n):
            for f in range(folds):
                at = b * blk + f * step
                proj += nt(gg[b], down[:, at : at + step])[f * rows : (f + 1) * rows]
        attr[...] = 16.0 / STEPS * activations.astype(F32) * proj
    for copy in sent:
        copy.wait_send()


def solution(mesh):
    n = mesh.shape["neur"]
    p, q = 4, n // 8
    m = p * q

    def local(activations, residual, down_weight, norm_gain, lens_weight, targets):
        rows, width = residual.shape
        neurons, vocab = down_weight.shape[0], lens_weight.shape[0]
        blk = width // n
        piece = (2 * rows, blk // 2) if blk % 256 == 0 else (rows + -rows % 16, blk)
        vmem, hbm = pl.BlockSpec(memory_space=pltpu.VMEM), pl.BlockSpec(memory_space=pl.ANY)
        sem = pltpu.SemaphoreType.DMA
        return pl.pallas_call(
            functools.partial(kernel, n, p, q),
            out_shape=(
                jax.ShapeDtypeStruct((rows, neurons), F32),
                jax.ShapeDtypeStruct((rows, STEPS), F32),
            ),
            in_specs=[vmem, vmem, vmem, vmem, hbm, hbm],
            out_specs=(vmem, vmem),
            scratch_shapes=[
                pltpu.VMEM(down_weight.shape, BF16),
                pltpu.VMEM(lens_weight.shape, BF16),
                pltpu.VMEM((m, rows, blk), F32),
                pltpu.VMEM((p, rows, blk), F32),
                pltpu.VMEM((2, m) + piece, BF16),
                pltpu.VMEM((2, m) + piece, BF16),
                pltpu.VMEM((2, q - 1, p) + piece, BF16),
                pltpu.VMEM((2, q - 1, p) + piece, BF16),
                pltpu.VMEM((2, p - 1) + piece, BF16),
                pltpu.VMEM((2, p - 1) + piece, BF16),
                pltpu.VMEM((n,) + piece, BF16),
                pltpu.VMEM((n,) + piece, BF16),
                pltpu.VMEM((n, rows, LANES), F32),
                pltpu.VMEM((STEPS, rows, vocab), F32),
                pltpu.VMEM((5, 2 * rows, LANES), F32),
                sem((3,)),
                sem((2, p + q - 1)),
                sem((2, p + q - 1)),
                sem((3, p + q - 1)),
                sem((3, p + q - 1)),
            ],
            compiler_params=pltpu.CompilerParams(
                collective_id=0, has_side_effects=True, vmem_limit_bytes=40 * 1024 * 1024
            ),
        )(activations, residual, norm_gain.astype(F32).reshape(1, width), targets.reshape(rows, 1),
          down_weight, lens_weight)

    placed = (P("grp", "neur"), P("grp", None), P("neur", None), P(), P("neur", None), P("grp"))
    return jax.shard_map(
        local,
        mesh=mesh,
        in_specs=placed,
        out_specs=(P("grp", "neur"), P("grp", None)),
        check_vma=False,
    )
```

time: 319 us -> 65.5 us (0.21)
  blocking collectives: 193 us -> 0 us
  waiting for transfers between devices: 91.5 us -> 0 us
  Pallas kernels: 0 us -> 56.9 us
  between operations: 14.2 us -> 0.64 us
  matrix products: 13.3 us -> 0 us
  local copies, waits for them, and re-layouts: 0.81 us -> 6.91 us
  other arithmetic: 4.44 us -> 0.72 us
    psum x2 -> x0, blocking collectives: 116 us -> none  [the longest x1 57.9 us: local(): lax.psum((jnp.dot(coefficient, lens_weight, preferred_element_type=jnp.fl...]
    reduce_scatter x1 -> x0, waiting for transfers between devices: 57.2 us -> none  [local(): lax.psum_scatter(lax.dot_general(down_weight, activations, (((0,), (1,)),...]
    pallas_call x0 -> x1, Pallas kernels: none -> 56.9 us  [local(): pl.pallas_call(functools.partial(kernel, n, p, q), out_shape=(jax.ShapeDt...]
    pmax x1 -> x0, blocking collectives: 53 us -> none  [local(): row_peak = lax.pmax(local_peak, 'neur')]
    psum x1 -> x0, waiting for transfers between devices: 34.3 us -> none  [local(): lax.psum((jnp.dot(coefficient, lens_weight, preferred_element_type=jnp.fl...]
    all_gather x1 -> x0, blocking collectives: 24.2 us -> none  [local(): update = lax.all_gather(column_piece, 'neur', axis=0, tiled=True).T]
    dot_general x8 -> x0, matrix products: 13.3 us -> none  [the longest x5 4.55 us: forward(): jnp.einsum('kpd,vd->kpv', normed, lens_weight, preferred_element_type=jnp...]
    unnamed x11 -> x10, local copies, waits for them, and re-layouts: 0.7 us -> 6.17 us
  transfers between devices with their start and end apart: 2 -> 0, of which waited for: 2 -> 0; matrix products, arithmetic and copies ran while one was open for 0% -> 0% of each run, Pallas kernels for 0% -> 0%
where the time goes in v1:
time: 65.5 us; the launch traced here: 65.2 us
  Pallas kernels  56.9 us (87%)
  local copies, waits for them, and re-layouts  6.91 us (11%)
  other arithmetic  0.72 us (1%)
    pallas_call x1, Pallas kernels, local(): pl.pallas_call(functools.partial(kernel, n, p, q), out_shape=(jax.ShapeDt...  56.9 us
    unnamed x10, local copies, waits for them, and re-layouts  6.17 us

profile of v1, /device:TPU:1, one launch (start us, length us, event | category | flops | bytes accessed | tf_op | source)
XLA Modules:
  0.0 65.2 jit_solution(2678163615284732286)
XLA Ops:
  0.6 0.7 %copy.8.tgt = s32[24,1]{1,0:T(8,128)S(1)} copy(s32[24,1]{0,1:T(1,128)} %bitcast.3) | data formatting | bytes 192 | tf_op jit(solution)/shard_map/reshape | solution.py:325
  1.4 0.7 %reshape.15 = f32[8192]{0:T(1024)S(1)} convert(bf16[8192]{0:T(1024)(128)(2,1)} %param.9) | non-fusion elementwise | flops 8192 | bytes 49152 | tf_op jit(solution)/shard_map/reshape | solution.py:325
  2.1 0.0 copy-start
  2.1 2.0 %copy-done = bf16[224,8192]{1,0:T(8,128)(2,1)S(1)} copy-done((bf16[224,8192]{1,0:T(8,128)(2,1)S(1)}, bf16[224,8192]{1,0:T(8,128)(2,1)}, u32[]{:S(2)}) %copy-start) | copy-done | bytes 3670040
  4.1 0.0 copy-start.1
  4.1 1.2 %copy-done.1 = bf16[64,8192]{1,0:T(8,128)(2,1)S(1)} copy-done((bf16[64,8192]{1,0:T(8,128)(2,1)S(1)}, bf16[64,8192]{1,0:T(8,128)(2,1)}, u32[]{:S(2)}) %copy-start.1) | copy-done | bytes 1048600
  5.3 0.0 copy-start.2
  5.4 1.0 %copy-done.2 = bf16[24,8192]{1,0:T(8,128)(2,1)S(1)} copy-done((bf16[24,8192]{1,0:T(8,128)(2,1)S(1)}, bf16[24,8192]{1,0:T(8,128)(2,1)}, u32[]{:S(2)}) %copy-start.2) | copy-done | bytes 393240
  6.3 0.0 copy-start.3
  6.3 0.7 %copy-done.3 = bf16[24,224]{1,0:T(8,128)(2,1)S(1)} copy-done((bf16[24,224]{1,0:T(8,128)(2,1)S(1)}, bf16[24,224]{1,0:T(8,128)(2,1)}, u32[]{:S(2)}) %copy-start.3) | copy-done | bytes 10776
  7.1 56.9 %shard_map.77 = (f32[24,224]{1,0:T(8,128)S(1)}, f32[24,20]{1,0:T(8,128)S(1)}) custom-call(bf16[24,224]{1,0:T(8,128)(2,1)S(1)} %copy-done.3, bf16[24,8192]{1,0:T(8,128)(2,1)S(1)} %copy-done.2, f32[1,8192]{1,0:T(1,128)S(1)} %bitcast.2, s32[24,1]{1,0:T(8,128)S(1)} %copy.8.tgt, bf16[224,8192]{1,0:T(8,128)(2,1)S(1)} %copy-done, bf16[64,8192]{1,0:T(8,128)(2,1)S(1)} %copy-done.1), custom_call_target="tpu_custom_call" | custom-call | tf_op jit(solution)/shard_map/pallas_call | solution.py:292
  64.0 0.6 copy.11
  64.6 0.6 copy.12
Async XLA Ops:
  2.1 2.0 %copy-start = (bf16[224,8192]{1,0:T(8,128)(2,1)S(1)}, bf16[224,8192]{1,0:T(8,128)(2,1)}, u32[]{:S(2)}) copy-start(bf16[224,8192]{1,0:T(8,128)(2,1)} %down_hbm.1) | copy-start | bytes 11010052
  4.1 1.2 %copy-start.1 = (bf16[64,8192]{1,0:T(8,128)(2,1)S(1)}, bf16[64,8192]{1,0:T(8,128)(2,1)}, u32[]{:S(2)}) copy-start(bf16[64,8192]{1,0:T(8,128)(2,1)} %lens_hbm.1) | copy-start | bytes 3145732
  5.3 1.0 %copy-start.2 = (bf16[24,8192]{1,0:T(8,128)(2,1)S(1)}, bf16[24,8192]{1,0:T(8,128)(2,1)}, u32[]{:S(2)}) copy-start(bf16[24,8192]{1,0:T(8,128)(2,1)} %res.1) | copy-start | bytes 1179652
  6.3 0.7 %copy-start.3 = (bf16[24,224]{1,0:T(8,128)(2,1)S(1)}, bf16[24,224]{1,0:T(8,128)(2,1)}, u32[]{:S(2)}) copy-start(bf16[24,224]{1,0:T(8,128)(2,1)} %act.1) | copy-start | bytes 32260

commit v2 on v0

v2 whole, which is shorter than its diff:
```python
import functools

import jax
import jax.numpy as jnp
from jax import lax
from jax.experimental import pallas as pl
from jax.experimental.pallas import tpu as pltpu
from jax.sharding import PartitionSpec as P

MESH = pl.DeviceIdType.MESH
STEPS = 20
EPS = 1e-05
F32, BF16 = jnp.float32, jnp.bfloat16
LANES = 128


def nt(x, y):
    return lax.dot_general(x, y, (((1,), (1,)), ((), ())), preferred_element_type=F32)


def loop(count, body):
    if count <= 8:
        for index in range(count):
            body(index)
    else:
        pl.loop(0, count)(body)


def pack(x):
    rows, cols = x.shape
    if cols % 256 == 0:
        return jnp.concatenate([x[:, : cols // 2], x[:, cols // 2 :]], axis=0).astype(BF16)
    return jnp.concatenate([x, jnp.zeros((-rows % 16, cols), F32)], axis=0).astype(BF16)


def unpack(y, rows):
    y = y.astype(F32)
    if y.shape[0] == 2 * rows:
        return jnp.concatenate([y[:rows], y[rows:]], axis=1)
    return y[:rows]


def fold(x):
    lane = lax.broadcasted_iota(jnp.int32, (8, LANES), 1)
    first = jnp.where(lane < LANES // 2, x[:8], pltpu.roll(x[8:16], LANES // 2, 1))
    return jnp.concatenate([first, x[16:24]], axis=0)


def unfold(y):
    return jnp.concatenate([y[:8], pltpu.roll(y[:8], LANES // 2, 1), y[8:16]], axis=0)


def kernel(n, chunks, act_hbm, res_hbm, gain_hbm, tgt_hbm, down_hbm, lens_hbm, attr, logp,
           act, res, rawgain, gain, tgt, down, lens, acc, s1, r1, s2, r2, ug, gg, st, part_s, part_r,
           ebuf, mats, projected, load_sem, rs_send, rs_recv, ag_send, ag_recv, pair_send, pair_recv):
    m = n // 2
    q = n // 8
    p = m // q
    rows, half = res.shape
    width = 2 * half
    vocab = 2 * lens.shape[1]
    span = half // chunks
    blk = span // m
    grp, me = lax.axis_index("grp"), lax.axis_index("neur")
    core = lax.rem(me, 2)
    spot = lax.rem(me // 2, q) * p + me // (2 * q)
    other = 1 - core

    def half_of(c):
        return pl.ds(pl.multiple_of(c * half, half), half)

    loads = [pltpu.make_async_copy(act_hbm, act, load_sem.at[0])]
    for slot in range(2 * chunks):
        at = (other, core)[slot // chunks] * half + (slot % chunks) * span
        cols = pl.ds(pl.multiple_of(at, span), span)
        loads.append(pltpu.make_async_copy(down_hbm.at[:, cols], down.at[:, cols], load_sem.at[1 + slot]))
    for slot, (src, dst) in enumerate(((lens_hbm.at[:, half_of(core)], lens.at[core]), (res_hbm.at[:, half_of(core)], res),
                                       (gain_hbm, rawgain), (tgt_hbm, tgt))):
        loads.append(pltpu.make_async_copy(src, dst, load_sem.at[1 + 2 * chunks + slot]))
    for load in loads:
        load.start()

    def dev(spot_at, c_at):
        return (grp, (lax.rem(spot_at, p) * q + spot_at // p) * 2 + c_at)

    core_peer = dev(spot, other)
    ahead = [lax.rem(spot + o, m) for o in range(m)]
    behind = [lax.rem(spot + m - o, m) for o in range(m)]
    barrier = pltpu.get_barrier_semaphore()
    for peer in [core_peer] + [dev(at, core) for at in ahead[1:]]:
        pl.semaphore_signal(barrier, inc=1, device_id=peer, device_id_type=MESH)
    pl.semaphore_wait(barrier, m)

    sent = []

    def send(src, dst, send_sem, recv_sem, peer):
        copy = pltpu.make_async_remote_copy(
            src_ref=src, dst_ref=dst, send_sem=send_sem, recv_sem=recv_sem,
            device_id=peer, device_id_type=MESH)
        copy.start()
        sent.append(copy)
        return copy

    heads = send(lens_hbm.at[:, half_of(other)], lens.at[core], pair_send.at[0], pair_recv.at[0], core_peer)

    def cols_of(c, j):
        return pl.ds(pl.multiple_of(c * span + j * blk, blk), blk)

    def send_sums(rd, c, part):
        ss, rs = rs_send.at[rd, c], rs_recv.at[rd, c]
        copies = []
        for o in range(1, m):
            s2[rd, c, o - 1] = pack(part(ahead[o]))
            copies.append(send(s2.at[rd, c, o - 1], r2.at[rd, c, o - 1], ss.at[o], rs.at[o], dev(ahead[o], core)))
        return copies

    def take_sums(rd, c, copies, total):
        for o in range(1, m):
            copies[o - 1].wait_recv()
            total = total + unpack(r2[rd, c, o - 1], rows)
        return total

    def gather(rd, c, own):
        ss, rs = ag_send.at[rd, c], ag_recv.at[rd, c]
        return [send(own, own, ss.at[o], rs.at[o], dev(ahead[o], core)) for o in range(1, m)]

    def split(x):
        high = x.astype(BF16).astype(F32)
        return jnp.concatenate([high, x - high], axis=0).astype(BF16)

    loads[0].wait()
    activations = act[...]

    def lane_sum(x):
        total = x[:, :LANES]
        for at in range(LANES, x.shape[1], LANES):
            total = total + x[:, at : at + LANES]
        return total

    def head(c):
        return lens[:, :, c * span : (c + 1) * span].reshape(vocab, span)

    def joined(buf, c, base):
        return jnp.concatenate([unpack(buf[c, base + j], rows) for j in range(m)], axis=1)

    mats[...] = jnp.zeros_like(mats)
    projected[...] = jnp.zeros_like(projected)
    acc_a, acc_b = mats.at[0], mats.at[1]
    sq_rr, sq_ru, sq_uu = (mats.at[2 + i, pl.ds(0, rows)] for i in range(3))

    def residual_terms():
        for load in loads[1 + 2 * chunks :]:
            load.wait()
        heads.wait_recv()
        mine = rawgain[core].astype(F32)
        for at in range(half // LANES):
            gain[:, at * LANES : (at + 1) * LANES] = mine[at : at + 1, :]
        for c in range(chunks):
            cols = slice(c * span, (c + 1) * span)
            base = res[:, cols].astype(F32)
            sq_rr[...] += lane_sum(base * base)
            acc_a[:, :vocab] += nt(split(gain[:, cols] * base), head(c))

    with jax.named_scope("update_sum"):
        def product(c, at, j):
            cols = pl.ds(pl.multiple_of(at * half + c * span + j * blk, blk), blk)
            return jnp.dot(activations, down[:, cols], preferred_element_type=F32)

        firsts = []
        for c in range(chunks):
            loads[1 + c].wait()
            for j in range(m):
                s1[c, j] = pack(product(c, other, j))
            firsts.append(send(s1.at[c], r1.at[c], pair_send.at[2 + c], pair_recv.at[2 + c], core_peer))
        for c in range(chunks):
            loads[1 + chunks + c].wait()
            for j in range(m):
                acc[c, j] = product(c, core, j)

        sums = []
        for c in range(chunks):
            firsts[c].wait_recv()

            def halved(j):
                return acc[c, j] + unpack(r1[c, j], rows)

            sums.append((send_sums(0, c, halved), halved(spot)))
        residual_terms()

    with jax.named_scope("update_gather"):
        updates, gathers = [], []
        for c in range(chunks):
            updates.append(take_sums(0, c, *sums[c]))
            ug[c, spot] = pack(updates[c])
            gathers.append(gather(0, c, ug.at[c, spot]))
        for c in range(chunks):
            for copy in gathers[c]:
                copy.wait_recv()
            cols = slice(c * span, (c + 1) * span)
            up = joined(ug, c, 0)
            sq_ru[...] += lane_sum(res[:, cols].astype(F32) * up)
            sq_uu[...] += lane_sum(up * up)
            acc_b[:, :vocab] += nt(split(gain[:, cols] * up), head(c))

    with jax.named_scope("pair_sum"):
        lane = lax.broadcasted_iota(jnp.int32, (rows, LANES), 1)
        part_s[0] = acc_a[:rows, :] + acc_a[rows:, :]
        part_s[1] = acc_b[:rows, :] + acc_b[rows:, :]
        norms = jnp.zeros((rows, LANES), F32)
        for i, sq in enumerate((sq_rr, sq_ru, sq_uu)):
            norms = jnp.where(lane == i, jnp.sum(sq[...], axis=1, keepdims=True), norms)
        part_s[2] = norms
        send(part_s, part_r, pair_send.at[1], pair_recv.at[1], core_peer).wait_recv()

    with jax.named_scope("softmax_parts"):
        a_log = (part_s[0] + part_r[0])[:, :vocab]
        b_log = (part_s[1] + part_r[1])[:, :vocab]
        norms = part_s[2] + part_r[2]
        rr = norms[:, 0:1] * (1.0 / width)
        ru = norms[:, 1:2] * (2.0 / width)
        uu = norms[:, 2:3] * (1.0 / width)
        alphas = (lane + 1).astype(F32) / STEPS
        live = lane < STEPS
        inv_root = 1.0 / jnp.sqrt(rr + alphas * ru + alphas * alphas * uu + EPS)
        inv_root = jnp.where(live, inv_root, 0.0)
        square = lax.broadcasted_iota(jnp.int32, (rows, rows), 0) == lax.broadcasted_iota(jnp.int32, (rows, rows), 1)
        target = jnp.sum(jnp.where(square, tgt[...].astype(F32), 0.0), axis=1, keepdims=True).astype(jnp.int32)
        hit = lax.broadcasted_iota(jnp.int32, (rows, vocab), 1) + (me // 2) * vocab == target
        a_hit = jnp.sum(jnp.where(hit, a_log, 0.0), axis=1, keepdims=True)
        b_hit = jnp.sum(jnp.where(hit, b_log, 0.0), axis=1, keepdims=True)
        peaks = jnp.zeros((rows, LANES), F32)
        packed = jnp.where(lane == 3 * STEPS, a_hit, jnp.where(lane == 3 * STEPS + 1, b_hit, 0.0))
        for k in range(STEPS):
            logits = (a_log + ((k + 1) / STEPS) * b_log) * inv_root[:, k : k + 1]
            peak = jnp.max(logits, axis=1, keepdims=True)
            grown = jnp.exp(logits - peak)
            ebuf[k] = grown
            peaks = jnp.where(lane == k, peak, peaks)
            packed = jnp.where(lane == STEPS + k, jnp.sum(grown, axis=1, keepdims=True), packed)
            packed = jnp.where(lane == 2 * STEPS + k, jnp.sum(grown * logits, axis=1, keepdims=True), packed)
        st[spot] = fold(jnp.where(live, peaks, packed))
    with jax.named_scope("softmax_gather"):
        for copy in gather(1, 0, st.at[spot]):
            copy.wait_recv()

    with jax.named_scope("softmax_whole"):
        top = st[0]
        for j in range(1, m):
            top = jnp.maximum(top, st[j])
        total, moment, plain = (jnp.zeros(top.shape, F32) for _ in range(3))
        for j in range(m):
            x = st[j]
            factor = jnp.exp(x - top)
            total += factor * pltpu.roll(x, LANES - STEPS, 1)
            moment += factor * pltpu.roll(x, LANES - 2 * STEPS, 1)
            plain += x
        top, total, moment, plain = unfold(top), unfold(total), unfold(moment), unfold(plain)
        total = jnp.where(live, total, 1.0)
        chosen = (plain[:, 3 * STEPS : 3 * STEPS + 1] + alphas * plain[:, 3 * STEPS + 1 : 3 * STEPS + 2]) * inv_root
        logp[...] = (chosen - top - jnp.log(total))[:, :STEPS]
        weight = (chosen - moment / total) * inv_root * inv_root * (1.0 / width)
        weight = jnp.where(live, weight, 0.0)
        first_sum = jnp.sum(weight, axis=1, keepdims=True)
        second_sum = jnp.sum(weight * alphas, axis=1, keepdims=True)
        scale = jnp.where(live, jnp.exp(peaks - top), 0.0) / total * inv_root
        coefficient = jnp.where(hit, jnp.sum(inv_root, axis=1, keepdims=True), 0.0)
        for k in range(STEPS):
            coefficient = coefficient - ebuf[k] * scale[:, k : k + 1]
        coefficient = coefficient.astype(BF16)

    with jax.named_scope("back_sum"):
        sums = []
        for c in range(chunks):
            def back_part(j):
                block = lens[:, :, cols_of(c, j)].reshape(vocab, blk)
                return jnp.dot(coefficient, block, preferred_element_type=F32)

            sums.append((send_sums(1, c, back_part), back_part(spot)))

    with jax.named_scope("gradient_gather"):
        gathers, relays = [], []

        def relay(c, j, slot):
            block = gg.at[c, core * m + j]
            relays[c].append(send(block, block, ag_send.at[2, c, slot], ag_recv.at[2, c, slot], core_peer))

        for c in range(chunks):
            back = take_sums(1, c, *sums[c])
            own = cols_of(c, spot)
            gg[c, core * m + spot] = pack(
                gain[:, own] * back - first_sum * res[:, own].astype(F32) - second_sum * updates[c])
            gathers.append(gather(2, c, gg.at[c, core * m + spot]))
            relays.append([])
            relay(c, spot, m)

        def project(c, at):
            cols = pl.ds(pl.multiple_of(at * half + c * span, span), span)
            projected[...] += nt(joined(gg, c, at * m).astype(BF16), down[:, cols])

        for c in range(chunks):
            for o in range(1, m):
                gathers[c][o - 1].wait_recv()
                relay(c, behind[o], m + o)
            project(c, core)
            for copy in relays[c]:
                copy.wait_recv()
            project(c, other)
    attr[...] = 16.0 / STEPS * activations.astype(F32) * projected[...]
    for copy in sent:
        copy.wait_send()


def solution(mesh):
    n = mesh.shape["neur"]
    m = n // 2

    def local(activations, residual, down_weight, norm_gain, lens_weight, targets):
        rows, width = residual.shape
        neurons, vocab = down_weight.shape[0], lens_weight.shape[0]
        chunks = 2 if width // n % 512 == 0 else 1
        blk = width // n // chunks
        piece = (2 * rows, blk // 2) if blk % 256 == 0 else (rows + -rows % 16, blk)
        vmem, hbm = pl.BlockSpec(memory_space=pltpu.VMEM), pl.BlockSpec(memory_space=pltpu.HBM)
        sem = pltpu.SemaphoreType.DMA
        half = width // 2
        gains = (2, half // LANES, LANES)
        return pl.pallas_call(
            functools.partial(kernel, n, chunks),
            out_shape=(
                jax.ShapeDtypeStruct((rows, neurons), F32),
                jax.ShapeDtypeStruct((rows, STEPS), F32),
            ),
            in_specs=[hbm] * 6,
            out_specs=(vmem, vmem),
            scratch_shapes=[
                pltpu.VMEM(activations.shape, BF16),
                pltpu.VMEM((rows, half), BF16),
                pltpu.VMEM(gains, BF16),
                pltpu.VMEM((1, half), F32),
                pltpu.VMEM((1, rows), jnp.int32),
                pltpu.VMEM(down_weight.shape, BF16),
                pltpu.VMEM((2, vocab, half), BF16),
                pltpu.VMEM((chunks, m, rows, blk), F32),
                pltpu.VMEM((chunks, m) + piece, BF16),
                pltpu.VMEM((chunks, m) + piece, BF16),
                pltpu.VMEM((2, chunks, m - 1) + piece, BF16),
                pltpu.VMEM((2, chunks, m - 1) + piece, BF16),
                pltpu.VMEM((chunks, m) + piece, BF16),
                pltpu.VMEM((chunks, n) + piece, BF16),
                pltpu.VMEM((m, 16, LANES), F32),
                pltpu.VMEM((3, rows, LANES), F32),
                pltpu.VMEM((3, rows, LANES), F32),
                pltpu.VMEM((STEPS, rows, 2 * vocab), F32),
                pltpu.VMEM((5, 2 * rows, LANES), F32),
                pltpu.VMEM((rows, neurons), F32),
                sem((5 + 2 * chunks,)),
                sem((2, chunks, m)),
                sem((2, chunks, m)),
                sem((3, chunks, n)),
                sem((3, chunks, n)),
                sem((2 + chunks,)),
                sem((2 + chunks,)),
            ],
            compiler_params=pltpu.CompilerParams(
                collective_id=0, has_side_effects=True, vmem_limit_bytes=40 * 1024 * 1024
            ),
        )(*[pltpu.with_memory_space_constraint(x, pltpu.HBM) for x in (activations, residual, norm_gain.reshape(gains), targets.reshape(1, rows), down_weight, lens_weight)])

    placed = (P("grp", "neur"), P("grp", None), P("neur", None), P(), P("neur", None), P("grp"))
    return jax.shard_map(
        local,
        mesh=mesh,
        in_specs=placed,
        out_specs=(P("grp", "neur"), P("grp", None)),
        check_vma=False,
    )
```

time: 319 us -> 44.9 us (0.14)
  blocking collectives: 193 us -> 0 us
  waiting for transfers between devices: 91.5 us -> 0 us
  Pallas kernels: 0 us -> 42.9 us
  between operations: 14.2 us -> 0.64 us
  matrix products: 13.3 us -> 0 us
  other arithmetic: 4.44 us -> 0 us
    psum x2 -> x0, blocking collectives: 116 us -> none  [the longest x1 57.9 us: local(): lax.psum((jnp.dot(coefficient, lens_weight, preferred_element_type=jnp.fl...]
    reduce_scatter x1 -> x0, waiting for transfers between devices: 57.2 us -> none  [local(): lax.psum_scatter(lax.dot_general(down_weight, activations, (((0,), (1,)),...]
    pmax x1 -> x0, blocking collectives: 53 us -> none  [local(): row_peak = lax.pmax(local_peak, 'neur')]
    pallas_call x0 -> x1, Pallas kernels: none -> 42.9 us  [local(): pl.pallas_call(functools.partial(kernel, n, chunks), out_shape=(jax.Shape...]
    psum x1 -> x0, waiting for transfers between devices: 34.3 us -> none  [local(): lax.psum((jnp.dot(coefficient, lens_weight, preferred_element_type=jnp.fl...]
    all_gather x1 -> x0, blocking collectives: 24.2 us -> none  [local(): update = lax.all_gather(column_piece, 'neur', axis=0, tiled=True).T]
    dot_general x8 -> x0, matrix products: 13.3 us -> none  [the longest x5 4.55 us: forward(): jnp.einsum('kpd,vd->kpv', normed, lens_weight, preferred_element_type=jnp...]
    reduce_sum x8 -> x0, other arithmetic: 4.02 us -> none  [the longest x5 3.2 us: forward(): root_mean = jnp.sqrt(jnp.mean(stream * stream, axis=2) + EPS)]
  transfers between devices with their start and end apart: 2 -> 0, of which waited for: 2 -> 0; matrix products, arithmetic and copies ran while one was open for 0% -> 0% of each run, Pallas kernels for 0% -> 0%
where the time goes in v2:
time: 44.9 us; the launch traced here: 44.7 us
  Pallas kernels  42.9 us (96%)
  local copies, waits for them, and re-layouts  1.21 us (3%)
  between operations  0.64 us (1%)
    pallas_call x1, Pallas kernels, local(): pl.pallas_call(functools.partial(kernel, n, chunks), out_shape=(jax.Shape...  42.9 us
    unnamed x2, local copies, waits for them, and re-layouts  1.21 us

profile of v2, /device:TPU:1, one launch (start us, length us, event | category | flops | bytes accessed | tf_op | source)
XLA Modules:
  0.0 44.7 jit_solution(3281904819370211089)
XLA Ops:
  0.6 42.9 %shard_map.77 = (f32[24,224]{1,0:T(8,128)S(1)}, f32[24,20]{1,0:T(8,128)S(1)}) custom-call(bf16[24,224]{1,0:T(8,128)(2,1)} %act_hbm.1, bf16[24,8192]{1,0:T(8,128)(2,1)} %res_hbm.1, bf16[2,32,128]{2,1,0:T(8,128)(2,1)} %bitcast.2, s32[1,24]{1,0:T(1,128)} %bitcast.3, bf16[224,8192]{1,0:T(8,128)(2,1)} %down_hbm.1, bf16[64,8192]{1,0:T(8,128)(2,1)} %lens_hbm.1), custom_call_target="tpu_custom_call" | custom-call | tf_op jit(solution)/shard_map/pallas_call | solution.py:327
  43.5 0.6 %copy.10 = f32[24,224]{1,0:T(8,128)} copy(f32[24,224]{1,0:T(8,128)S(1)} %get-tuple-element.4) | data formatting | bytes 43008
  44.1 0.6 %copy.11 = f32[24,20]{1,0:T(8,128)} copy(f32[24,20]{1,0:T(8,128)S(1)} %get-tuple-element.5) | data formatting | bytes 3840

commit v3 on v2

--- a/solution.py
+++ b/solution.py
@@ -16,14 +16,6 @@
 
 def nt(x, y):
     return lax.dot_general(x, y, (((1,), (1,)), ((), ())), preferred_element_type=F32)
-
-
-def loop(count, body):
-    if count <= 8:
-        for index in range(count):
-            body(index)
-    else:
-        pl.loop(0, count)(body)
 
 
 def pack(x):
@@ -89,9 +81,13 @@
     barrier = pltpu.get_barrier_semaphore()
     for peer in [core_peer] + [dev(at, core) for at in ahead[1:]]:
         pl.semaphore_signal(barrier, inc=1, device_id=peer, device_id_type=MESH)
-    pl.semaphore_wait(barrier, m)
 
     sent = []
+
+    def flush():
+        for copy in sent:
+            copy.wait_send()
+        sent.clear()
 
     def send(src, dst, send_sem, recv_sem, peer):
         copy = pltpu.make_async_remote_copy(
@@ -101,7 +97,6 @@
         sent.append(copy)
         return copy
 
-    heads = send(lens_hbm.at[:, half_of(other)], lens.at[core], pair_send.at[0], pair_recv.at[0], core_peer)
 
     def cols_of(c, j):
         return pl.ds(pl.multiple_of(c * span + j * blk, blk), blk)
@@ -148,7 +143,7 @@
     acc_a, acc_b = mats.at[0], mats.at[1]
     sq_rr, sq_ru, sq_uu = (mats.at[2 + i, pl.ds(0, rows)] for i in range(3))
 
-    def residual_terms():
+    def residual_terms(heads):
         for load in loads[1 + 2 * chunks :]:
             load.wait()
         heads.wait_recv()
@@ -171,7 +166,10 @@
             loads[1 + c].wait()
             for j in range(m):
                 s1[c, j] = pack(product(c, other, j))
+            if c == 0:
+                pl.semaphore_wait(barrier, m)
             firsts.append(send(s1.at[c], r1.at[c], pair_send.at[2 + c], pair_recv.at[2 + c], core_peer))
+        heads = send(lens_hbm.at[:, half_of(other)], lens.at[core], pair_send.at[0], pair_recv.at[0], core_peer)
         for c in range(chunks):
             loads[1 + chunks + c].wait()
             for j in range(m):
@@ -185,7 +183,7 @@
                 return acc[c, j] + unpack(r1[c, j], rows)
 
             sums.append((send_sums(0, c, halved), halved(spot)))
-        residual_terms()
+        residual_terms(heads)
 
     with jax.named_scope("update_gather"):
         updates, gathers = [], []
@@ -240,7 +238,11 @@
             packed = jnp.where(lane == 2 * STEPS + k, jnp.sum(grown * logits, axis=1, keepdims=True), packed)
         st[spot] = fold(jnp.where(live, peaks, packed))
     with jax.named_scope("softmax_gather"):
-        for copy in gather(1, 0, st.at[spot]):
+        copies = gather(1, 0, st.at[spot])
+        for copy in sent[: -len(copies)]:
+            copy.wait_send()
+        del sent[: -len(copies)]
+        for copy in copies:
             copy.wait_recv()
 
     with jax.named_scope("softmax_whole"):
@@ -280,34 +282,29 @@
     with jax.named_scope("gradient_gather"):
         gathers, relays = [], []
 
-        def relay(c, j, slot):
-            block = gg.at[c, core * m + j]
-            relays[c].append(send(block, block, ag_send.at[2, c, slot], ag_recv.at[2, c, slot], core_peer))
-
         for c in range(chunks):
             back = take_sums(1, c, *sums[c])
             own = cols_of(c, spot)
             gg[c, core * m + spot] = pack(
                 gain[:, own] * back - first_sum * res[:, own].astype(F32) - second_sum * updates[c])
             gathers.append(gather(2, c, gg.at[c, core * m + spot]))
-            relays.append([])
-            relay(c, spot, m)
 
         def project(c, at):
             cols = pl.ds(pl.multiple_of(at * half + c * span, span), span)
             projected[...] += nt(joined(gg, c, at * m).astype(BF16), down[:, cols])
 
         for c in range(chunks):
-            for o in range(1, m):
-                gathers[c][o - 1].wait_recv()
-                relay(c, behind[o], m + o)
+            for copy in gathers[c]:
+                copy.wait_recv()
+            block = gg.at[c, pl.ds(core * m, m)]
+            relays.append(send(block, block, ag_send.at[2, c, m], ag_recv.at[2, c, m], core_peer))
             project(c, core)
-            for copy in relays[c]:
-                copy.wait_recv()
+            if c == 0:
+                flush()
+            relays[c].wait_recv()
             project(c, other)
     attr[...] = 16.0 / STEPS * activations.astype(F32) * projected[...]
-    for copy in sent:
-        copy.wait_send()
+    flush()
 
 
 def solution(mesh):

time: 44.9 us -> 44 us (0.980)
  Pallas kernels: 42.9 us -> 42 us
    pallas_call x1, Pallas kernels: 42.9 us -> 42 us  [local(): pl.pallas_call(functools.partial(kernel, n, chunks), out_shape=(jax.Shape...]
where the time goes in v3:
time: 44 us; the launch traced here: 43.8 us
  Pallas kernels  42 us (95%)
  local copies, waits for them, and re-layouts  1.21 us (3%)
  between operations  0.64 us (1%)
    pallas_call x1, Pallas kernels, local(): pl.pallas_call(functools.partial(kernel, n, chunks), out_shape=(jax.Shape...  42 us
    unnamed x2, local copies, waits for them, and re-layouts  1.21 us

profile of v3, /device:TPU:1, one launch (start us, length us, event | category | flops | bytes accessed | tf_op | source)
XLA Modules:
  0.0 43.8 jit_solution(14380570635441726638)
XLA Ops:
  0.6 42.0 %shard_map.77 = (f32[24,224]{1,0:T(8,128)S(1)}, f32[24,20]{1,0:T(8,128)S(1)}) custom-call(bf16[24,224]{1,0:T(8,128)(2,1)} %act_hbm.1, bf16[24,8192]{1,0:T(8,128)(2,1)} %res_hbm.1, bf16[2,32,128]{2,1,0:T(8,128)(2,1)} %bitcast.2, s32[1,24]{1,0:T(1,128)} %bitcast.3, bf16[224,8192]{1,0:T(8,128)(2,1)} %down_hbm.1, bf16[64,8192]{1,0:T(8,128)(2,1)} %lens_hbm.1), custom_call_target="tpu_custom_call" | custom-call | tf_op jit(solution)/shard_map/pallas_call | solution.py:324
  42.6 0.6 %copy.10 = f32[24,224]{1,0:T(8,128)} copy(f32[24,224]{1,0:T(8,128)S(1)} %get-tuple-element.4) | data formatting | bytes 43008
  43.2 0.6 %copy.11 = f32[24,20]{1,0:T(8,128)} copy(f32[24,20]{1,0:T(8,128)S(1)} %get-tuple-element.5) | data formatting | bytes 3840

commit v4 on v3

--- a/solution.py
+++ b/solution.py
@@ -44,7 +44,7 @@
 
 def kernel(n, chunks, act_hbm, res_hbm, gain_hbm, tgt_hbm, down_hbm, lens_hbm, attr, logp,
            act, res, rawgain, gain, tgt, down, lens, acc, s1, r1, s2, r2, ug, gg, st, part_s, part_r,
-           ebuf, mats, projected, load_sem, rs_send, rs_recv, ag_send, ag_recv, pair_send, pair_recv):
+           ebuf, mats, scores, projected, load_sem, rs_send, rs_recv, ag_send, ag_recv, pair_send, pair_recv):
     m = n // 2
     q = n // 8
     p = m // q
@@ -140,7 +140,7 @@
 
     mats[...] = jnp.zeros_like(mats)
     projected[...] = jnp.zeros_like(projected)
-    acc_a, acc_b = mats.at[0], mats.at[1]
+    scores[...] = jnp.zeros_like(scores)
     sq_rr, sq_ru, sq_uu = (mats.at[2 + i, pl.ds(0, rows)] for i in range(3))
 
     def residual_terms(heads):
@@ -154,7 +154,7 @@
             cols = slice(c * span, (c + 1) * span)
             base = res[:, cols].astype(F32)
             sq_rr[...] += lane_sum(base * base)
-            acc_a[:, :vocab] += nt(split(gain[:, cols] * base), head(c))
+            scores[0, :, : 2 * rows] += nt(head(c), split(gain[:, cols] * base))
 
     with jax.named_scope("update_sum"):
         def product(c, at, j):
@@ -198,12 +198,13 @@
             up = joined(ug, c, 0)
             sq_ru[...] += lane_sum(res[:, cols].astype(F32) * up)
             sq_uu[...] += lane_sum(up * up)
-            acc_b[:, :vocab] += nt(split(gain[:, cols] * up), head(c))
+            scores[1, :, : 2 * rows] += nt(head(c), split(gain[:, cols] * up))
 
     with jax.named_scope("pair_sum"):
         lane = lax.broadcasted_iota(jnp.int32, (rows, LANES), 1)
-        part_s[0] = acc_a[:rows, :] + acc_a[rows:, :]
-        part_s[1] = acc_b[:rows, :] + acc_b[rows:, :]
+        for i in range(2):
+            turned = scores[i].T
+            part_s[i] = turned[:rows] + turned[rows : 2 * rows]
         norms = jnp.zeros((rows, LANES), F32)
         for i, sq in enumerate((sq_rr, sq_ru, sq_uu)):
             norms = jnp.where(lane == i, jnp.sum(sq[...], axis=1, keepdims=True), norms)
@@ -291,7 +292,7 @@
 
         def project(c, at):
             cols = pl.ds(pl.multiple_of(at * half + c * span, span), span)
-            projected[...] += nt(joined(gg, c, at * m).astype(BF16), down[:, cols])
+            projected[: down.shape[0], :rows] += nt(down[:, cols], joined(gg, c, at * m).astype(BF16))
 
         for c in range(chunks):
             for copy in gathers[c]:
@@ -303,7 +304,7 @@
                 flush()
             relays[c].wait_recv()
             project(c, other)
-    attr[...] = 16.0 / STEPS * activations.astype(F32) * projected[...]
+    attr[...] = 16.0 / STEPS * activations.astype(F32) * projected[...].T[:rows, : down.shape[0]]
     flush()
 
 
@@ -349,7 +350,8 @@
                 pltpu.VMEM((3, rows, LANES), F32),
                 pltpu.VMEM((STEPS, rows, 2 * vocab), F32),
                 pltpu.VMEM((5, 2 * rows, LANES), F32),
-                pltpu.VMEM((rows, neurons), F32),
+                pltpu.VMEM((2, 2 * vocab, LANES), F32),
+                pltpu.VMEM((neurons + -neurons % LANES, LANES), F32),
                 sem((5 + 2 * chunks,)),
                 sem((2, chunks, m)),
                 sem((2, chunks, m)),

time: 44 us -> 43.8 us (level)
  no operation moved by 1% of the time
where the time goes in v4:
time: 43.8 us; the launch traced here: 43.6 us
  Pallas kernels  41.8 us (95%)
  local copies, waits for them, and re-layouts  1.21 us (3%)
  between operations  0.64 us (1%)
    pallas_call x1, Pallas kernels, local(): pl.pallas_call(functools.partial(kernel, n, chunks), out_shape=(jax.Shape...  41.8 us
    unnamed x2, local copies, waits for them, and re-layouts  1.21 us

profile of v4, /device:TPU:1, one launch (start us, length us, event | category | flops | bytes accessed | tf_op | source)
XLA Modules:
  0.0 43.6 jit_solution(8697189844565029792)
XLA Ops:
  0.6 41.8 %shard_map.77 = (f32[24,224]{1,0:T(8,128)S(1)}, f32[24,20]{1,0:T(8,128)S(1)}) custom-call(bf16[24,224]{1,0:T(8,128)(2,1)} %act_hbm.1, bf16[24,8192]{1,0:T(8,128)(2,1)} %res_hbm.1, bf16[2,32,128]{2,1,0:T(8,128)(2,1)} %bitcast.2, s32[1,24]{1,0:T(1,128)} %bitcast.3, bf16[224,8192]{1,0:T(8,128)(2,1)} %down_hbm.1, bf16[64,8192]{1,0:T(8,128)(2,1)} %lens_hbm.1), custom_call_target="tpu_custom_call" | custom-call | tf_op jit(solution)/shard_map/pallas_call | solution.py:325
  42.4 0.6 %copy.10 = f32[24,224]{1,0:T(8,128)} copy(f32[24,224]{1,0:T(8,128)S(1)} %get-tuple-element.4) | data formatting | bytes 43008
  43.0 0.6 %copy.11 = f32[24,20]{1,0:T(8,128)} copy(f32[24,20]{1,0:T(8,128)S(1)} %get-tuple-element.5) | data formatting | bytes 3840
